TPU v7x, 32 devices: a whole 2x2x4 slice. The times are simulated.
32 devices in a mesh: grp: 2 (over y), vv: 4 (over z), oo: 2 (over core), rep: 2 (over x).
Axes of the slice: x: 2, y: 2, z: 4, core: 2. Of those that a mesh axis runs over, the one named last changes fastest.
Arguments:
- amplitudes: bfloat16 [8192, 4096], P(('grp', 'vv'), ('oo', 'rep')), parts along dimension 0, may hold values from -6 to 6
- integrals: bfloat16 [8, 4096, 16384], P(None, ('oo', 'rep'), ('grp', 'vv')), parts along dimension 2, may hold values from -0.125 to 0.125
- occ_irrep: int32 [64], replicated, may hold values from 0 to 7
- virt_count: int32 [8], replicated, may hold values from 1 to 128, 640 in all
- c_irrep: int32 [32], replicated, may hold values from 0 to 7
- a_irrep: int32 [64], replicated, may hold values from 0 to 7
Outputs:
- ladder: bfloat16 [4096, 16384], P(('oo', 'rep'), ('grp', 'vv')), parts along dimension 1
There are 2 independent parts, one for each index of `grp`. A program takes and returns all parts, laid end to end along the dimension named above; an argument that names none is the same for every part. Nothing has to cross between parts.
Inputs may be any that keep to these rules, and one draw needn't show every extreme that they name: `virt_count`: the counts of the 8 irreps sum to 640; the largest is exactly 128.
All inputs are finite; a program needn't handle non-finite values.
Results may differ from a plain program's by a relative error of at most 0.01.
Values may be sent and summed in bfloat16 or wider, within the bound.
A program may use at most 192 MiB of HBM per device.

v0:
```python
import jax
import jax.numpy as jnp
from jax import lax
from jax.sharding import PartitionSpec as P

O = 64
VMAX = 128
TILE = 256


def lookup(labels_in, table_values):
    hits = labels_in[..., None] == jnp.arange(table_values.shape[0], dtype=jnp.int32)
    return jnp.sum(jnp.where(hits, table_values, 0), axis=-1, dtype=jnp.int32)


def slot_valid(slot_index, slot_irrep, virt_count):
    orbital_slot = slot_index // VMAX
    position = slot_index % VMAX
    slot_label = lookup(orbital_slot, slot_irrep)
    irreps_all = jnp.arange(8, dtype=jnp.int32)[:, None]
    needed = jnp.bitwise_xor(irreps_all, slot_label[None, :])
    return position[None, :] < lookup(needed, virt_count)


def pair_irreps(occ_irrep, pair_count):
    pair_ids = jnp.arange(pair_count, dtype=jnp.int32)
    return jnp.bitwise_xor(lookup(pair_ids // O, occ_irrep), lookup(pair_ids % O, occ_irrep))


def tile_layout(row_irrep, tile_rows, tile_total):
    labels_all = jnp.arange(8, dtype=jnp.int32)
    member = (row_irrep[:, None] == labels_all[None, :]).astype(jnp.int32)
    counts = jnp.sum(member, axis=0, dtype=jnp.int32)
    before = jnp.cumsum(member, axis=0, dtype=jnp.int32) - member
    rank_in = jnp.sum(before * member, axis=1, dtype=jnp.int32)
    tile_counts = (counts + tile_rows - 1) // tile_rows
    tile_ends = jnp.cumsum(tile_counts, dtype=jnp.int32)
    tile_starts = tile_ends - tile_counts
    position = jnp.sum(member * tile_starts[None, :], axis=1, dtype=jnp.int32) * tile_rows + rank_in
    slots_total = tile_total * tile_rows
    row_numbers = jnp.arange(row_irrep.shape[0], dtype=jnp.int32)
    source = jnp.zeros((slots_total,), jnp.int32).at[position].set(row_numbers)
    filled = jnp.zeros((slots_total,), jnp.int32).at[position].set(jnp.ones_like(row_numbers))
    tile_ids = jnp.arange(tile_total, dtype=jnp.int32)
    passed = (tile_ends[None, :] <= tile_ids[:, None]).astype(jnp.int32)
    tile_irrep = jnp.minimum(jnp.sum(passed, axis=1, dtype=jnp.int32), 7)
    return (position, source, filled, tile_irrep)


def ladder_tiles(row_block_all, integrals, k_valid, q_valid, layout, tile_rows, tile_total):
    position, source, filled, tile_irrep = layout
    zero_value = jnp.zeros((), integrals.dtype)

    def one_tile(state_in, tile_id):
        source_rows = lax.dynamic_slice_in_dim(source, tile_id * tile_rows, tile_rows)
        filled_now = lax.dynamic_slice_in_dim(filled, tile_id * tile_rows, tile_rows)
        row_block = jnp.where(filled_now[:, None] > 0, row_block_all[source_rows], zero_value)
        irrep_now = tile_irrep[tile_id]
        weights = jnp.where(
            k_valid[irrep_now][:, None] & q_valid[irrep_now][None, :],
            integrals[irrep_now],
            zero_value,
        )
        product = jnp.dot(row_block, weights, preferred_element_type=jnp.float32)
        return (
            state_in,
            lax.optimization_barrier(product.astype(jnp.bfloat16)).astype(jnp.float32),
        )

    _, outputs = lax.scan(one_tile, jnp.int32(0), jnp.arange(tile_total, dtype=jnp.int32))
    flat = outputs.reshape(tile_total * tile_rows, integrals.shape[2])
    return flat[position]


def local(amplitudes, integrals, occ_irrep, virt_count, c_irrep, a_irrep):
    n_rep = lax.axis_size("rep")
    k_local = amplitudes.shape[1]
    q_local = integrals.shape[2]
    pair_total = amplitudes.shape[0] * lax.axis_size("vv")
    k_first = (lax.axis_index("oo") * n_rep + lax.axis_index("rep")) * k_local
    q_first = lax.axis_index("vv") * q_local
    k_valid = slot_valid(k_first + jnp.arange(k_local, dtype=jnp.int32), c_irrep, virt_count)
    q_valid = slot_valid(q_first + jnp.arange(q_local, dtype=jnp.int32), a_irrep, virt_count)
    row_irrep = pair_irreps(occ_irrep, pair_total)
    tile_total = pair_total // TILE + 8
    layout = tile_layout(row_irrep, TILE, tile_total)
    all_rows = lax.all_gather(amplitudes, "vv", axis=0, tiled=True)
    ladder_term = ladder_tiles(all_rows, integrals, k_valid, q_valid, layout, TILE, tile_total)
    summed = lax.psum_scatter(
        ladder_term.astype(jnp.bfloat16), ("oo", "rep"), scatter_dimension=0, tiled=True
    )
    return summed


def solution(mesh):
    placed = (
        P(("grp", "vv"), ("oo", "rep")),
        P(None, ("oo", "rep"), ("grp", "vv")),
        P(),
        P(),
        P(),
        P(),
    )
    return jax.shard_map(
        local,
        mesh=mesh,
        in_specs=placed,
        out_specs=P(("oo", "rep"), ("grp", "vv")),
        check_vma=False,
    )
```

profile of v0, /device:TPU:1, one launch (start us, length us, event | category | flops | bytes accessed | tf_op | source)
XLA Modules:
  0.0 745.8 jit_solution(7637152503756847877)
XLA Ops:
  11.9 15.5 %scatter_custom_fusion = s32[6144]{0:T(1024)S(1)} fusion(s32[4096]{0:T(1024)S(1)} %bitcast.48, s32[4096]{0:T(1024)S(1)} %ne.154, s32[]{:T(128)} %constant.129.clone.1), kind=kCustom, calls=%fused_computation.70 | custom fusion | bytes 24580 | tf_op jit(solution)/shard_map/scatter | solution.py:43
  27.5 15.7 %scatter_custom_fusion.1 = s32[6144]{0:T(1024)S(1)} fusion(s32[4096]{0:T(1024)S(1)} %bitcast.49, s32[4096]{0:T(1024)S(1)} %iota.74, s32[]{:T(128)} %constant.129.clone.1), kind=kCustom, calls=%fused_computation.68 | custom fusion | bytes 24580 | tf_op jit(solution)/shard_map/scatter | solution.py:42
  46.7 114.2 %all-gather.2.cloned.1.call-done = bf16[4096,1024]{1,0:T(8,128)(2,1)} async-done(((bf16[1024,1024]{1,0:T(8,128)(2,1)}), bf16[4096,1024]{1,0:T(8,128)(2,1)}) %all-gather.2.cloned.1.call-update) | async-done | bytes 8388624 | tf_op jit(solution)/shard_map/all_gather | solution.py:87
  160.9 411.0 %while.10 = (s32[]{:T(128)}, bf16[24,256,2048]{2,1,0:T(8,128)(2,1)}, s32[24]{0:T(128)S(1)}, s32[6144]{0:T(1024)S(1)}, s32[6144]{0:T(1024)S(1)}, /*index=5*/bf16[...) while((s32[]{:T(128)}, ...), condition=%wide.region_16.17_spmd, body=%wide.region_15.16_spmd.sunk | while | flops 1079248896 | bytes 9981235 | solution.py:70
  166.9 6.0 gather_fusion
  184.0 6.0 gather_fusion
  201.1 6.0 gather_fusion
  218.3 6.0 gather_fusion
  235.4 6.0 gather_fusion
  252.5 6.0 gather_fusion
  269.6 6.0 gather_fusion
  286.8 6.0 gather_fusion
  303.9 6.0 gather_fusion
  321.1 6.0 gather_fusion
  338.1 6.0 gather_fusion
  355.3 6.0 gather_fusion
  372.4 6.0 gather_fusion
  389.5 6.0 gather_fusion
  406.6 6.0 gather_fusion
  475.2 6.0 gather_fusion
  509.4 6.0 gather_fusion
  543.6 6.0 gather_fusion
  571.9 42.7 %gather_fusion.1 = bf16[4096,2048]{1,0:T(8,128)(2,1)} fusion(bf16[6144,2048]{1,0:T(8,128)(2,1)} %bitcast.45, s32[4096]{0:T(1024)S(1)} %broadcast_clamp_fusion), kind=kCustom, calls=%fused_computation.1 | custom fusion | bytes 33570816 | tf_op jit(solution)/shard_map/gather | solution.py:72
  614.7 124.3 %reduce-scatter.2.cloned.1.call-done = bf16[1024,2048]{1,0:T(8,128)(2,1)} async-done(((bf16[4096,2048]{1,0:T(8,128)(2,1)}), bf16[1024,2048]{1,0:T(8,128)(2,1)}) %reduce-scatter.2.cloned.1.call-update) | async-done | bytes 4194320 | tf_op jit(solution)/shard_map/reduce_scatter | solution.py:89
  (260 shorter events, 202.3 us)
Async XLA Ops:
  6.5 154.4 %all-gather.2.cloned.1.call-start = ((), (), s32[]{:S(2)}) async-start(), calls=%async_computation.1 | async-start | bytes 10485760 | tf_op jit(solution)/shard_map/all_gather | solution.py:87
  7.3 731.7 %reduce-scatter.2.cloned.1.call-start = ((), (), s32[]{:S(2)}) async-start(), calls=%async_computation.2 | async-start | bytes 20971520 | tf_op jit(solution)/shard_map/reduce_scatter | solution.py:89
Sparse Core Ops, SparseCore 0:
  8.9 151.9 all-gather.1
  614.8 124.0 reduce-scatter.1
where the time goes:
time: 750 us; the launch traced here: 746 us
  local copies, waits for them, and re-layouts  251 us (33%)
  waiting for transfers between devices  239 us (32%)
  loops' own time  109 us (15%)
  matrix products  95.6 us (13%)
  other arithmetic  37.5 us (5%)
  between operations  13.6 us (2%)
    gather x24, local copies, waits for them, and re-layouts, one_tile(): row_block_all[source_rows]  144 us
    reduce_scatter x1, waiting for transfers between devices, local(): lax.psum_scatter(ladder_term.astype(jnp.bfloat16), ('oo', 'rep'), scatter...  124 us
    all_gather x1, waiting for transfers between devices, local(): all_rows = lax.all_gather(amplitudes, 'vv', axis=0, tiled=True)  114 us
    another operation x1, loops' own time, ladder_tiles(): lax.scan(one_tile, jnp.int32(0), jnp.arange(tile_total, dtype=jnp.int32))  109 us
    dot_general x24, matrix products, one_tile(): product = jnp.dot(row_block, weights, preferred_element_type=jnp.float32)  95.6 us
    gather x1, local copies, waits for them, and re-layouts, ladder_tiles(): return flat[position]  42.7 us
    dynamic_update_slice x24, other arithmetic, ladder_tiles(): lax.scan(one_tile, jnp.int32(0), jnp.arange(tile_total, dtype=jnp.int32))  25.7 us
    scatter x1, local copies, waits for them, and re-layouts, tile_layout(): source = jnp.zeros((slots_total,), jnp.int32).at[position].set(row_numbers)  15.7 us
  transfers between devices with their start and end apart: 2, of which 2 were waited for; matrix products, arithmetic and copies ran while one was open for 5% of the time, Pallas kernels for 0%

commit v1 on v0

--- a/solution.py
+++ b/solution.py
@@ -1,6 +1,10 @@
+import functools
+
 import jax
 import jax.numpy as jnp
 from jax import lax
+from jax.experimental import pallas as pl
+from jax.experimental.pallas import tpu as pltpu
 from jax.sharding import PartitionSpec as P
 
 O = 64
@@ -92,6 +96,315 @@
     return summed
 
 
+SUB = 512
+T = 128
+NT = SUB // T
+NP = NT + 7
+NH = 8
+QC = 512
+STRIDE = 64
+MESH = pl.DeviceIdType.MESH
+
+
+def place(step, zz, side):
+    middle = ((step + 2) // 4) % 2
+    blk_mid = middle * 2 * (step % 2) + (1 - middle) * (1 + 2 * (step // 4))
+    half_mid = middle * (step // 2 - 1) + (1 - middle) * (step % 2)
+    near = zz * blk_mid + (1 - zz) * (step // 2)
+    half = zz * half_mid + (1 - zz) * (step % 2)
+    blk = near + side * (3 - 2 * near)
+    return near, blk, half
+
+
+def ladder_kernel(
+    tab, src_ref, pos_ref, seg_ref, kval_ref, qval_ref, a_hbm, v_hbm, out_hbm,
+    v_all, a_all, a_now, unsort, pairs, tiles, part, core_in, rep_in,
+    v_sem, a_sem, z_recv, own_send, fwd_send, core_send, core_recv, rep_send, rep_recv, out_sem,
+):
+    z = lax.axis_index("vv")
+    core = lax.axis_index("oo")
+    rep = lax.axis_index("rep")
+    side = z // 2
+    zz = z + side * (3 - 2 * z)
+    outer = (1 - side) * (z - 1) + side * (z + 1)
+    inner = (1 - side) * (z + 1) + side * (z - 1)
+
+    def z_copy(h, target, send):
+        return pltpu.make_async_remote_copy(
+            src_ref=a_all.at[h], dst_ref=a_all.at[h], send_sem=send, recv_sem=z_recv.at[h],
+            device_id={"vv": target}, device_id_type=MESH,
+        )
+
+    def core_copy(step):
+        _, blk, half = place(step, zz, side)
+        slot = (blk % 2) * 2 + half
+        return pltpu.make_async_remote_copy(
+            src_ref=part.at[step % 2], dst_ref=core_in.at[slot],
+            send_sem=core_send.at[step % 2], recv_sem=core_recv.at[slot],
+            device_id={"oo": 1 - core}, device_id_type=MESH,
+        )
+
+    def rep_copy(slot, half):
+        return pltpu.make_async_remote_copy(
+            src_ref=core_in.at[slot], dst_ref=rep_in.at[half],
+            send_sem=rep_send.at[half], recv_sem=rep_recv.at[half],
+            device_id={"rep": 1 - rep}, device_id_type=MESH,
+        )
+
+    a_copies = [
+        pltpu.make_async_copy(a_hbm.at[pl.ds(k * SUB, SUB)], part.at[k, :, pl.ds(0, a_hbm.shape[1])], a_sem.at[k])
+        for k in range(2)
+    ]
+    for copy in a_copies:
+        copy.start()
+    v_copies = [
+        pltpu.make_async_copy(v_hbm.at[r, :, pl.ds(c * QC, QC)], v_all.at[r, c], v_sem.at[r, c])
+        for c in range(v_all.shape[1])
+        for r in range(8)
+    ]
+    for copy in v_copies:
+        copy.start()
+
+    barrier = pltpu.get_barrier_semaphore()
+    pl.semaphore_signal(barrier, inc=1, device_id={"vv": inner}, device_id_type=MESH)
+    pl.semaphore_signal(barrier, inc=1, device_id={"oo": 1 - core}, device_id_type=MESH)
+    pl.semaphore_signal(barrier, inc=1, device_id={"rep": 1 - rep}, device_id_type=MESH)
+
+    @pl.when(zz == 1)
+    def _():
+        pl.semaphore_signal(barrier, inc=1, device_id={"vv": outer}, device_id_type=MESH)
+
+    pl.semaphore_wait(barrier, 3 + zz)
+
+    pairs[0] = jnp.zeros_like(pairs[0])
+    for k in range(2):
+        a_copies[k].wait()
+        h = z * 2 + k
+        rows = lax.broadcasted_iota(jnp.int32, (SUB, SUB), 0)
+        order = (rows == pos_ref[h]).astype(jnp.float32).astype(jnp.bfloat16)
+        lanes = lax.broadcasted_iota(jnp.int32, (SUB, 128), 0)
+        segs = seg_ref[h]
+        label = ((lanes >= segs[0:1]) & (lanes < segs[1:2])).astype(jnp.float32).astype(jnp.bfloat16)
+        keep = jnp.dot(label, kval_ref[...], preferred_element_type=jnp.float32)
+        moved = jnp.dot(order, part[k, :, 0:a_hbm.shape[1]], preferred_element_type=jnp.float32)
+        a_all[h] = (moved * keep).astype(jnp.bfloat16)
+        z_copy(h, inner, own_send.at[k]).start()
+
+        @pl.when(zz == 1)
+        def _():
+            z_copy(h, outer, own_send.at[2 + k]).start()
+
+    for copy in v_copies:
+        copy.wait()
+
+    def compute(h, slot):
+        for t in range(NT):
+            a_now[t] = a_all[h, t * T:(t + 1) * T, :]
+        rows = lax.broadcasted_iota(jnp.int32, (SUB, SUB), 0)
+        unsort[...] = (rows == src_ref[h]).astype(jnp.float32).astype(jnp.bfloat16)
+
+        def columns(chunk, carry):
+            q0 = pl.multiple_of(chunk * QC, QC)
+
+            def pair(p, carry):
+                base = h * STRIDE + p * 4
+                tile = tab[base]
+                irrep = tab[base + 1]
+                left = a_now[tile]
+                product = jnp.dot(left, v_all[irrep, chunk], preferred_element_type=jnp.float32)
+                product = jnp.where(qval_ref[irrep, chunk] > 0, product, 0.0)
+                place_in = lax.broadcasted_iota(jnp.int32, (T, QC), 0) + tile * T
+                mine = (place_in >= tab[base + 2]) & (place_in < tab[base + 3])
+                merged = jnp.where(mine, product, pairs[p].astype(jnp.float32))
+                pairs[p + 1] = merged.astype(jnp.bfloat16)
+                return carry
+
+            lax.fori_loop(0, NP, pair, 0)
+            for t in range(NT):
+                tiles[t * T:(t + 1) * T, :] = pairs[tab[h * STRIDE + 48 + t] + 1]
+            back = jnp.dot(unsort[...], tiles[...], preferred_element_type=jnp.float32)
+            part[slot, :, pl.ds(q0, QC)] = back.astype(jnp.bfloat16)
+            return carry
+
+        lax.fori_loop(0, v_all.shape[1], columns, 0)
+
+    def finish(step):
+        _, blk, half = place(step, zz, side)
+        slot = (blk % 2) * 2 + half
+
+        @pl.when(blk // 2 == core)
+        def _():
+            core_copy(step).wait_recv()
+
+            def add(c, carry):
+                at = pl.ds(pl.multiple_of(c * 64, 64), 64)
+                total = core_in[slot, at, :].astype(jnp.float32) + part[step % 2, at, :].astype(jnp.float32)
+                core_in[slot, at, :] = total.astype(jnp.bfloat16)
+                return carry
+
+            lax.fori_loop(0, SUB // 64, add, 0)
+
+            @pl.when(blk % 2 != rep)
+            def _():
+                rep_copy(slot, half).start()
+
+    def body(step, carry):
+        near, blk, half = place(step, zz, side)
+        h = blk * 2 + half
+
+        @pl.when(near != zz)
+        def _():
+            z_copy(h, inner, own_send.at[0]).wait_recv()
+
+        @pl.when((zz == 1) & (near == 0))
+        def _():
+            z_copy(h, inner, fwd_send.at[h]).start()
+
+        @pl.when((zz == 1) & (near > 1))
+        def _():
+            z_copy(h, outer, fwd_send.at[h]).start()
+
+        @pl.when(step >= 2)
+        def _():
+            _, before, _ = place(step - 2, zz, side)
+
+            @pl.when(before // 2 != core)
+            def _():
+                core_copy(step - 2).wait_send()
+
+        compute(h, step % 2)
+
+        @pl.when(blk // 2 != core)
+        def _():
+            core_copy(step).start()
+
+        @pl.when(step >= 1)
+        def _():
+            finish(step - 1)
+
+        return carry
+
+    lax.fori_loop(0, NH, body, 0)
+    finish(NH - 1)
+
+    for step in (NH - 2, NH - 1):
+        _, blk, _ = place(step, zz, side)
+
+        @pl.when(blk // 2 != core)
+        def _():
+            core_copy(step).wait_send()
+
+    outs = []
+    for half in range(2):
+        rep_copy(rep * 2 + half, half).wait_recv()
+
+        def add(c, carry):
+            at = pl.ds(pl.multiple_of(c * 64, 64), 64)
+            total = core_in[rep * 2 + half, at, :].astype(jnp.float32) + rep_in[half, at, :].astype(jnp.float32)
+            rep_in[half, at, :] = total.astype(jnp.bfloat16)
+            return carry
+
+        lax.fori_loop(0, SUB // 64, add, 0)
+        copy = pltpu.make_async_copy(rep_in.at[half], out_hbm.at[pl.ds(half * SUB, SUB)], out_sem.at[half])
+        copy.start()
+        outs.append(copy)
+    for half in range(2):
+        rep_copy((1 - rep) * 2 + half, half).wait_send()
+        z_copy(z * 2 + half, inner, own_send.at[half]).wait_send()
+
+    @pl.when(zz == 1)
+    def _():
+        for half in range(2):
+            z_copy(z * 2 + half, outer, own_send.at[2 + half]).wait_send()
+            for near in (0, 2, 3):
+                h = (near + side * (3 - 2 * near)) * 2 + half
+                z_copy(h, outer, fwd_send.at[h]).wait_send()
+
+    for copy in outs:
+        copy.wait()
+
+
+def exclusive(values, axis):
+    return jnp.cumsum(values, axis=axis, dtype=jnp.int32) - values
+
+
+def layout_tables(row_irrep):
+    labels = row_irrep.reshape(NH, 1, SUB)
+    member = (labels == jnp.arange(8, dtype=jnp.int32)[None, :, None])
+    upper = jnp.arange(SUB)[:, None] < jnp.arange(SUB)[None, :]
+    before = jnp.einsum(
+        "hrn,nm->hrm", member.astype(jnp.bfloat16), upper.astype(jnp.bfloat16), preferred_element_type=jnp.float32
+    ).astype(jnp.int32)
+    counts = jnp.sum(member, axis=2, dtype=jnp.int32)
+    r8 = jnp.arange(8)
+    ends = jnp.sum(jnp.where(r8[None, :, None] >= r8[None, None, :], counts[:, None, :], 0), axis=2, dtype=jnp.int32)
+    starts = ends - counts
+    pos = jnp.sum(jnp.where(member, before + starts[:, :, None], 0), axis=1, dtype=jnp.int32)
+    seats = jnp.arange(SUB, dtype=jnp.int32)
+    src = jnp.sum(
+        jnp.where(pos[:, None, :] == seats[None, :, None], seats[None, None, :], 0), axis=2, dtype=jnp.int32
+    )
+    cut = jnp.minimum(ends[:, :7] // T, NT - 1)
+    turn = jnp.arange(7, dtype=jnp.int32)[None, :] + cut
+    steps = jnp.arange(NP, dtype=jnp.int32)
+    irrep = jnp.sum((turn[:, None, :] < steps[None, :, None]).astype(jnp.int32), axis=2, dtype=jnp.int32)
+    tile = steps[None, :] - irrep
+    pick = irrep[:, :, None] == r8[None, None, :]
+    first = jnp.sum(jnp.where(pick, starts[:, None, :], 0), axis=2, dtype=jnp.int32)
+    last = jnp.sum(jnp.where(pick, ends[:, None, :], 0), axis=2, dtype=jnp.int32)
+    t4 = jnp.arange(NT, dtype=jnp.int32)
+    done = t4[None, :] + jnp.sum((cut[:, None, :] <= t4[None, :, None]).astype(jnp.int32), axis=2, dtype=jnp.int32)
+    done = jnp.where(t4[None, :] == NT - 1, NP - 1, done)
+    rows = jnp.stack([tile, irrep, first, last], axis=2).reshape(NH, NP * 4)
+    tab = jnp.concatenate(
+        [rows, jnp.zeros((NH, 48 - NP * 4), jnp.int32), done, jnp.zeros((NH, STRIDE - 48 - NT), jnp.int32)], axis=1
+    ).reshape(NH * STRIDE)
+    seg = jnp.zeros((NH, 2, 128), jnp.int32).at[:, 0, :8].set(starts).at[:, 1, :8].set(ends)
+    return tab, src.reshape(NH, 1, SUB), pos.reshape(NH, 1, SUB), seg
+
+
+def fused(amplitudes, integrals, occ_irrep, virt_count, c_irrep, a_irrep):
+    k_local = amplitudes.shape[1]
+    q_local = integrals.shape[2]
+    k_first = (lax.axis_index("oo") * lax.axis_size("rep") + lax.axis_index("rep")) * k_local
+    q_first = lax.axis_index("vv") * q_local
+    k_valid = slot_valid(k_first + jnp.arange(k_local, dtype=jnp.int32), c_irrep, virt_count)
+    q_valid = slot_valid(q_first + jnp.arange(q_local, dtype=jnp.int32), a_irrep, virt_count)
+    row_irrep = jnp.bitwise_xor(occ_irrep[:, None], occ_irrep[None, :]).reshape(-1)
+    tab, src, pos, seg = layout_tables(row_irrep)
+    kval = jnp.pad(k_valid.astype(jnp.bfloat16), ((0, 120), (0, 0)))
+    qval = q_valid.astype(jnp.float32).reshape(8, q_local // QC, 1, QC)
+    vmem = pl.BlockSpec(memory_space=pltpu.VMEM)
+    hbm = pl.BlockSpec(memory_space=pl.ANY)
+    dma = pltpu.SemaphoreType.DMA
+    bf16 = jnp.bfloat16
+    return pl.pallas_call(
+        ladder_kernel,
+        out_shape=jax.ShapeDtypeStruct((2 * SUB, q_local), bf16),
+        in_specs=[pl.BlockSpec(memory_space=pltpu.SMEM)] + [vmem] * 5 + [hbm] * 2,
+        out_specs=hbm,
+        scratch_shapes=[
+            pltpu.VMEM((8, q_local // QC, k_local, QC), bf16),
+            pltpu.VMEM((NH, SUB, k_local), bf16),
+            pltpu.VMEM((NT, T, k_local), bf16),
+            pltpu.VMEM((SUB, SUB), bf16),
+            pltpu.VMEM((NP + 1, T, QC), bf16),
+            pltpu.VMEM((SUB, QC), bf16),
+            pltpu.VMEM((2, SUB, q_local), bf16),
+            pltpu.VMEM((4, SUB, q_local), bf16),
+            pltpu.VMEM((2, SUB, q_local), bf16),
+            dma((8, q_local // QC)), dma((2,)), dma((NH,)), dma((4,)), dma((NH,)),
+            dma((2,)), dma((4,)), dma((2,)), dma((2,)), dma((2,)),
+        ],
+        compiler_params=pltpu.CompilerParams(
+            collective_id=0, has_side_effects=True, vmem_limit_bytes=64 * 1024 * 1024 - 256 * 1024
+        ),
+        cost_estimate=pl.CostEstimate(
+            flops=2 * NH * NP * T * k_local * q_local, bytes_accessed=40 * 1024 * 1024, transcendentals=0
+        ),
+    )(tab, src, pos, seg, kval, qval, amplitudes, integrals)
+
+
 def solution(mesh):
     placed = (
         P(("grp", "vv"), ("oo", "rep")),
@@ -101,8 +414,10 @@
         P(),
         P(),
     )
+    shape = dict(mesh.shape)
+    same = (shape['vv'], shape['oo'], shape['rep'], shape['grp']) == (4, 2, 2, 2)
     return jax.shard_map(
-        local,
+        fused if same else local,
         mesh=mesh,
         in_specs=placed,
         out_specs=P(("oo", "rep"), ("grp", "vv")),

time: 750 us -> 247 us (0.33)
  local copies, waits for them, and re-layouts: 251 us -> 9.22 us
  waiting for transfers between devices: 239 us -> 0 us
  Pallas kernels: 0 us -> 226 us
  loops' own time: 109 us -> 0 us
  matrix products: 95.6 us -> 0.24 us
  other arithmetic: 37.5 us -> 6.62 us
  between operations: 13.6 us -> 0.17 us
    pallas_call x0 -> x1, Pallas kernels: none -> 226 us  [fused(): pl.pallas_call(ladder_kernel, out_shape=jax.ShapeDtypeStruct((2 * SUB, q_...]
    gather x25 -> x0, local copies, waits for them, and re-layouts: 187 us -> none  [the longest x24 144 us: one_tile(): row_block_all[source_rows]]
    reduce_scatter x1 -> x0, waiting for transfers between devices: 124 us -> none  [local(): lax.psum_scatter(ladder_term.astype(jnp.bfloat16), ('oo', 'rep'), scatter...]
    all_gather x1 -> x0, waiting for transfers between devices: 114 us -> none  [local(): all_rows = lax.all_gather(amplitudes, 'vv', axis=0, tiled=True)]
    another operation x1 -> x0, loops' own time: 109 us -> none  [ladder_tiles(): lax.scan(one_tile, jnp.int32(0), jnp.arange(tile_total, dtype=jnp.int32))]
    dot_general x24 -> x1, matrix products: 95.6 us -> 0.24 us  [layout_tables(): jnp.einsum('hrn,nm->hrm', member.astype(jnp.bfloat16), upper.astype(jnp.b...]
    dynamic_slice x96 -> x0, local copies, waits for them, and re-layouts: 32 us -> none  [the longest x24 15.5 us: ladder_tiles(): lax.scan(one_tile, jnp.int32(0), jnp.arange(tile_total, dtype=jnp.int32))]
    scatter x2, local copies, waits for them, and re-layouts: 31.3 us -> 0.26 us  [layout_tables(): jnp.zeros((NH, 2, 128), jnp.int32).at[:, 0, :8].set(starts).at[:, 1, :8]]
  transfers between devices with their start and end apart: 2 -> 0, of which waited for: 2 -> 0; matrix products, arithmetic and copies ran while one was open for 5% -> 0% of each run, Pallas kernels for 0% -> 0%
where the time goes in v1:
time: 247 us; the launch traced here: 242 us
  Pallas kernels  226 us (91%)
  local copies, waits for them, and re-layouts  9.22 us (4%)
  other arithmetic  6.62 us (3%)
    pallas_call x1, Pallas kernels, fused(): pl.pallas_call(ladder_kernel, out_shape=jax.ShapeDtypeStruct((2 * SUB, q_...  226 us

profile of v1, /device:TPU:1, one launch (start us, length us, event | category | flops | bytes accessed | tf_op | source)
XLA Modules:
  0.0 242.4 jit_solution(14845083555485243361)
XLA Ops:
  0.2 0.7 xor.62
  0.9 0.7 xor.59
  1.7 0.7 select_reduce_fusion.4
  2.4 0.8 select_reduce_fusion.2
  3.3 0.8 select_reduce_fusion.3
  4.3 0.2 convert_reduce_fusion
  4.5 0.2 select_reduce_fusion.7
  4.7 0.2 fusion.2
  5.0 0.3 scatter.9.seg_ref
  5.3 0.1 copy.32
  5.4 0.1 select_reduce_fusion.6
  5.6 0.1 copy.34
  5.8 0.1 copy.36
  5.8 0.1 copy.33
  6.1 0.7 reshape.282.tab
  6.8 0.6 broadcast_in_dim.158.pos_ref
  7.4 1.0 select_reduce_fusion
  8.4 0.6 reshape.283.src_ref
  9.0 0.9 select_reduce_fusion.1
  9.9 0.1 reduce_sum.131
  10.0 0.7 compare_convert_fusion.qval_ref
  10.7 0.7 pad_convert_fusion.kval_ref
  11.5 226.1 %shard_map.64 = bf16[1024,2048]{1,0:T(8,128)(2,1)} custom-call(s32[512]{0:T(512)} %reshape.282.tab, s32[8,1,512]{2,1,0:T(1,128)} %reshape.283.src_ref, s32[8,1,512]{2,1,0:T(1,128)} %broadcast_in_dim.158.pos_ref, s32[8,2,128]{2,1,0:T(2,128)} %copy-done, bf16[128,1024]{1,0:T(8,128)(2,1)} %pad_convert_fusion.kval_ref, ...), custom_call_target="tpu_custom_call" | custom-call | flops 47244640256 | bytes 41943040 | tf_op jit(solution)/shard_map/pallas_call | solution.py:381
  237.6 4.8 %copy.41 = bf16[1024,2048]{1,0:T(8,128)(2,1)} copy(bf16[1024,2048]{1,0:T(8,128)(2,1)} %shard_map.64) | data formatting | bytes 8388608
  (30 shorter events, 0.8 us)
Async XLA Ops:
  5.3 6.2 %copy-start = (s32[8,2,128]{2,1,0:T(2,128)}, s32[8,2,128]{2,1,0:T(2,128)S(1)}, u32[]{:S(2)}) copy-start(s32[8,2,128]{2,1,0:T(2,128)S(1)} %scatter.9.seg_ref) | copy-start | bytes 24580

commit v2 on v1

--- a/solution.py
+++ b/solution.py
@@ -96,30 +96,29 @@
     return summed
 
 
-SUB = 512
-T = 128
+SUB = 1024
+HALF = 512
+T = 256
 NT = SUB // T
 NP = NT + 7
-NH = 8
+NH = 4
 QC = 512
+NQ = 4
 STRIDE = 64
 MESH = pl.DeviceIdType.MESH
 
 
-def place(step, zz, side):
-    middle = ((step + 2) // 4) % 2
-    blk_mid = middle * 2 * (step % 2) + (1 - middle) * (1 + 2 * (step // 4))
-    half_mid = middle * (step // 2 - 1) + (1 - middle) * (step % 2)
-    near = zz * blk_mid + (1 - zz) * (step // 2)
-    half = zz * half_mid + (1 - zz) * (step % 2)
-    blk = near + side * (3 - 2 * near)
-    return near, blk, half
+def place(step, zz, side, swap):
+    turn = step // 4
+    late = turn // 2
+    near = late * (turn + swap * (5 - 2 * turn)) + (1 - late) * (turn + zz * (1 - 2 * turn))
+    return near, near + side * (3 - 2 * near), step % 4
 
 
 def ladder_kernel(
     tab, src_ref, pos_ref, seg_ref, kval_ref, qval_ref, a_hbm, v_hbm, out_hbm,
-    v_all, a_all, a_now, unsort, pairs, tiles, part, core_in, rep_in,
-    v_sem, a_sem, z_recv, own_send, fwd_send, core_send, core_recv, rep_send, rep_recv, out_sem,
+    v_all, a_all, a_now, pairs, tiles, part, core_in, rep_in,
+    v_sem, a_sem, z_recv, z_send, core_send, core_recv, rep_send, rep_recv, out_sem,
 ):
     z = lax.axis_index("vv")
     core = lax.axis_index("oo")
@@ -128,38 +127,49 @@
     zz = z + side * (3 - 2 * z)
     outer = (1 - side) * (z - 1) + side * (z + 1)
     inner = (1 - side) * (z + 1) + side * (z - 1)
-
-    def z_copy(h, target, send):
+    swap = 1 - rep - side + 2 * rep * side
+
+    def z_copy(near, half, target, send):
+        blk = near + side * (3 - 2 * near)
+        at = a_all.at[blk, pl.ds(half * HALF, HALF)]
         return pltpu.make_async_remote_copy(
-            src_ref=a_all.at[h], dst_ref=a_all.at[h], send_sem=send, recv_sem=z_recv.at[h],
+            src_ref=at, dst_ref=at, send_sem=z_send.at[send], recv_sem=z_recv.at[blk, half],
             device_id={"vv": target}, device_id_type=MESH,
         )
 
+    def arrive(near, half):
+        z_copy(near, half, inner, 0).wait_recv()
+
+    sends = [(1, 0, inner, 0), (1, 1, inner, 1), (0, 0, inner, 2), (0, 1, inner, 3), (1, 0, outer, 4), (1, 1, outer, 5)]
+    sends += [(2, 0, outer, 6), (2, 1, outer, 7), (3, 0, outer, 8), (3, 1, outer, 9)]
+
+    def send(k):
+        z_copy(*sends[k]).start()
+
     def core_copy(step):
-        _, blk, half = place(step, zz, side)
-        slot = (blk % 2) * 2 + half
+        _, blk, qc = place(step, zz, side, swap)
+        slot = (blk % 2) * NQ + qc
         return pltpu.make_async_remote_copy(
             src_ref=part.at[step % 2], dst_ref=core_in.at[slot],
             send_sem=core_send.at[step % 2], recv_sem=core_recv.at[slot],
             device_id={"oo": 1 - core}, device_id_type=MESH,
         )
 
-    def rep_copy(slot, half):
+    def rep_copy(slot, qc):
         return pltpu.make_async_remote_copy(
-            src_ref=core_in.at[slot], dst_ref=rep_in.at[half],
-            send_sem=rep_send.at[half], recv_sem=rep_recv.at[half],
+            src_ref=core_in.at[slot], dst_ref=rep_in.at[qc],
+            send_sem=rep_send.at[qc], recv_sem=rep_recv.at[qc],
             device_id={"rep": 1 - rep}, device_id_type=MESH,
         )
 
     a_copies = [
-        pltpu.make_async_copy(a_hbm.at[pl.ds(k * SUB, SUB)], part.at[k, :, pl.ds(0, a_hbm.shape[1])], a_sem.at[k])
-        for k in range(2)
+        pltpu.make_async_copy(a_hbm.at[pl.ds(t * T, T)], a_now.at[t], a_sem.at[t]) for t in range(NT)
     ]
     for copy in a_copies:
         copy.start()
     v_copies = [
         pltpu.make_async_copy(v_hbm.at[r, :, pl.ds(c * QC, QC)], v_all.at[r, c], v_sem.at[r, c])
-        for c in range(v_all.shape[1])
+        for c in range(NQ)
         for r in range(8)
     ]
     for copy in v_copies:
@@ -177,102 +187,164 @@
     pl.semaphore_wait(barrier, 3 + zz)
 
     pairs[0] = jnp.zeros_like(pairs[0])
-    for k in range(2):
-        a_copies[k].wait()
-        h = z * 2 + k
-        rows = lax.broadcasted_iota(jnp.int32, (SUB, SUB), 0)
-        order = (rows == pos_ref[h]).astype(jnp.float32).astype(jnp.bfloat16)
-        lanes = lax.broadcasted_iota(jnp.int32, (SUB, 128), 0)
-        segs = seg_ref[h]
+    for copy in a_copies:
+        copy.wait()
+    segs = seg_ref[z]
+    for t in range(NT):
+        rows = lax.broadcasted_iota(jnp.int32, (T, SUB), 0) + t * T
+        order = (rows == pos_ref[z]).astype(jnp.float32).astype(jnp.bfloat16)
+        lanes = lax.broadcasted_iota(jnp.int32, (T, 128), 0) + t * T
         label = ((lanes >= segs[0:1]) & (lanes < segs[1:2])).astype(jnp.float32).astype(jnp.bfloat16)
         keep = jnp.dot(label, kval_ref[...], preferred_element_type=jnp.float32)
-        moved = jnp.dot(order, part[k, :, 0:a_hbm.shape[1]], preferred_element_type=jnp.float32)
-        a_all[h] = (moved * keep).astype(jnp.bfloat16)
-        z_copy(h, inner, own_send.at[k]).start()
-
-        @pl.when(zz == 1)
-        def _():
-            z_copy(h, outer, own_send.at[2 + k]).start()
-
-    for copy in v_copies:
-        copy.wait()
-
-    def compute(h, slot):
+        raw = a_now[...].reshape(SUB, a_now.shape[2])
+        moved = jnp.dot(order, raw, preferred_element_type=jnp.float32)
+        a_all[z, t * T:(t + 1) * T, :] = (moved * keep).astype(jnp.bfloat16)
+        if t % 2 == 1:
+            half = t // 2
+
+            @pl.when(zz == 0)
+            def _():
+                z_copy(0, half, inner, half).start()
+
+            @pl.when(zz == 1)
+            def _():
+                send(4 + half)
+
+            if half == 0:
+
+                @pl.when(zz == 1)
+                def _():
+                    send(0)
+
+            else:
+
+                @pl.when((zz == 1) & (swap == 1))
+                def _():
+                    send(1)
+
+    def load(blk):
         for t in range(NT):
-            a_now[t] = a_all[h, t * T:(t + 1) * T, :]
-        rows = lax.broadcasted_iota(jnp.int32, (SUB, SUB), 0)
-        unsort[...] = (rows == src_ref[h]).astype(jnp.float32).astype(jnp.bfloat16)
-
-        def columns(chunk, carry):
-            q0 = pl.multiple_of(chunk * QC, QC)
-
-            def pair(p, carry):
-                base = h * STRIDE + p * 4
-                tile = tab[base]
-                irrep = tab[base + 1]
-                left = a_now[tile]
-                product = jnp.dot(left, v_all[irrep, chunk], preferred_element_type=jnp.float32)
-                product = jnp.where(qval_ref[irrep, chunk] > 0, product, 0.0)
-                place_in = lax.broadcasted_iota(jnp.int32, (T, QC), 0) + tile * T
-                mine = (place_in >= tab[base + 2]) & (place_in < tab[base + 3])
-                merged = jnp.where(mine, product, pairs[p].astype(jnp.float32))
-                pairs[p + 1] = merged.astype(jnp.bfloat16)
-                return carry
-
-            lax.fori_loop(0, NP, pair, 0)
-            for t in range(NT):
-                tiles[t * T:(t + 1) * T, :] = pairs[tab[h * STRIDE + 48 + t] + 1]
-            back = jnp.dot(unsort[...], tiles[...], preferred_element_type=jnp.float32)
-            part[slot, :, pl.ds(q0, QC)] = back.astype(jnp.bfloat16)
+            a_now[t] = a_all[blk, t * T:(t + 1) * T, :]
+
+    def compute(blk, chunk, slot):
+        def pair(p, carry):
+            base = blk * STRIDE + p * 4
+            tile = tab[base]
+            irrep = tab[base + 1]
+            product = jnp.dot(a_now[tile], v_all[irrep, chunk], preferred_element_type=jnp.float32)
+            product = jnp.where(qval_ref[irrep, chunk] > 0, product, 0.0)
+            place_in = lax.broadcasted_iota(jnp.int32, (T, QC), 0) + tile * T
+            mine = (place_in >= tab[base + 2]) & (place_in < tab[base + 3])
+            merged = jnp.where(mine, product, pairs[p].astype(jnp.float32))
+            pairs[p + 1] = merged.astype(jnp.bfloat16)
             return carry
 
-        lax.fori_loop(0, v_all.shape[1], columns, 0)
+        lax.fori_loop(0, NP, pair, 0)
+        for t in range(NT):
+            tiles[t * T:(t + 1) * T, :] = pairs[tab[blk * STRIDE + 48 + t] + 1]
+        for t in range(NT):
+            rows = lax.broadcasted_iota(jnp.int32, (T, SUB), 0) + t * T
+            unsort = (rows == src_ref[blk]).astype(jnp.float32).astype(jnp.bfloat16)
+            back = jnp.dot(unsort, tiles[...], preferred_element_type=jnp.float32)
+            part[slot, t * T:(t + 1) * T, :] = back.astype(jnp.bfloat16)
 
     def finish(step):
-        _, blk, half = place(step, zz, side)
-        slot = (blk % 2) * 2 + half
+        _, blk, qc = place(step, zz, side, swap)
+        slot = (blk % 2) * NQ + qc
 
         @pl.when(blk // 2 == core)
         def _():
             core_copy(step).wait_recv()
 
             def add(c, carry):
-                at = pl.ds(pl.multiple_of(c * 64, 64), 64)
+                at = pl.ds(pl.multiple_of(c * 128, 128), 128)
                 total = core_in[slot, at, :].astype(jnp.float32) + part[step % 2, at, :].astype(jnp.float32)
                 core_in[slot, at, :] = total.astype(jnp.bfloat16)
                 return carry
 
-            lax.fori_loop(0, SUB // 64, add, 0)
+            lax.fori_loop(0, SUB // 128, add, 0)
 
             @pl.when(blk % 2 != rep)
             def _():
-                rep_copy(slot, half).start()
+                rep_copy(slot, qc).start()
+
+    def arrivals(step):
+        @pl.when((zz == 0) & (step % 4 == 0) & (step > 0))
+        def _():
+            near, _, _ = place(step, zz, side, swap)
+            arrive(near, 0)
+            arrive(near, 1)
+
+        @pl.when((zz == 1) & (step == 4))
+        def _():
+            arrive(0, 0)
+            send(2)
+            arrive(2, 0)
+
+            @pl.when(swap == 0)
+            def _():
+                send(6)
+
+            arrive(0, 1)
+            send(3)
+
+            @pl.when(swap == 0)
+            def _():
+                send(1)
+                arrive(3 - 1, 1)
+                send(7)
+
+            @pl.when(swap == 1)
+            def _():
+                arrive(3, 0)
+                send(8)
+
+        @pl.when((zz == 1) & (swap == 1) & (step == 8))
+        def _():
+            arrive(3, 1)
+            send(9)
+
+        @pl.when((zz == 1) & (swap == 1) & (step == 11))
+        def _():
+            send(6)
+
+        @pl.when((zz == 1) & (swap == 1) & (step == 12))
+        def _():
+            arrive(2, 1)
+            send(7)
+
+        @pl.when((zz == 1) & (swap == 0) & (step == 10))
+        def _():
+            arrive(3, 0)
+            send(8)
+
+        @pl.when((zz == 1) & (swap == 0) & (step == 12))
+        def _():
+            arrive(3, 1)
+            send(9)
 
     def body(step, carry):
-        near, blk, half = place(step, zz, side)
-        h = blk * 2 + half
-
-        @pl.when(near != zz)
-        def _():
-            z_copy(h, inner, own_send.at[0]).wait_recv()
-
-        @pl.when((zz == 1) & (near == 0))
-        def _():
-            z_copy(h, inner, fwd_send.at[h]).start()
-
-        @pl.when((zz == 1) & (near > 1))
-        def _():
-            z_copy(h, outer, fwd_send.at[h]).start()
+        _, blk, qc = place(step, zz, side, swap)
+        arrivals(step)
+
+        @pl.when(step == 0)
+        def _():
+            for copy in v_copies:
+                copy.wait()
 
         @pl.when(step >= 2)
         def _():
-            _, before, _ = place(step - 2, zz, side)
+            _, before, _ = place(step - 2, zz, side, swap)
 
             @pl.when(before // 2 != core)
             def _():
                 core_copy(step - 2).wait_send()
 
-        compute(h, step % 2)
+        @pl.when(qc == 0)
+        def _():
+            load(blk)
+
+        compute(blk, qc, step % 2)
 
         @pl.when(blk // 2 != core)
         def _():
@@ -284,41 +356,42 @@
 
         return carry
 
-    lax.fori_loop(0, NH, body, 0)
-    finish(NH - 1)
-
-    for step in (NH - 2, NH - 1):
-        _, blk, _ = place(step, zz, side)
+    lax.fori_loop(0, NH * NQ, body, 0)
+    finish(NH * NQ - 1)
+
+    for step in (NH * NQ - 2, NH * NQ - 1):
+        _, blk, _ = place(step, zz, side, swap)
 
         @pl.when(blk // 2 != core)
         def _():
             core_copy(step).wait_send()
 
     outs = []
-    for half in range(2):
-        rep_copy(rep * 2 + half, half).wait_recv()
+    for qc in range(NQ):
+        rep_copy(rep * NQ + qc, qc).wait_recv()
 
         def add(c, carry):
-            at = pl.ds(pl.multiple_of(c * 64, 64), 64)
-            total = core_in[rep * 2 + half, at, :].astype(jnp.float32) + rep_in[half, at, :].astype(jnp.float32)
-            rep_in[half, at, :] = total.astype(jnp.bfloat16)
+            at = pl.ds(pl.multiple_of(c * 128, 128), 128)
+            total = core_in[rep * NQ + qc, at, :].astype(jnp.float32) + rep_in[qc, at, :].astype(jnp.float32)
+            rep_in[qc, at, :] = total.astype(jnp.bfloat16)
             return carry
 
-        lax.fori_loop(0, SUB // 64, add, 0)
-        copy = pltpu.make_async_copy(rep_in.at[half], out_hbm.at[pl.ds(half * SUB, SUB)], out_sem.at[half])
+        lax.fori_loop(0, SUB // 128, add, 0)
+        copy = pltpu.make_async_copy(rep_in.at[qc], out_hbm.at[:, pl.ds(qc * QC, QC)], out_sem.at[qc])
         copy.start()
         outs.append(copy)
-    for half in range(2):
-        rep_copy((1 - rep) * 2 + half, half).wait_send()
-        z_copy(z * 2 + half, inner, own_send.at[half]).wait_send()
+    for qc in range(NQ):
+        rep_copy((1 - rep) * NQ + qc, qc).wait_send()
+
+    @pl.when(zz == 0)
+    def _():
+        for half in range(2):
+            z_copy(0, half, inner, half).wait_send()
 
     @pl.when(zz == 1)
     def _():
-        for half in range(2):
-            z_copy(z * 2 + half, outer, own_send.at[2 + half]).wait_send()
-            for near in (0, 2, 3):
-                h = (near + side * (3 - 2 * near)) * 2 + half
-                z_copy(h, outer, fwd_send.at[h]).wait_send()
+        for k in range(10):
+            z_copy(*sends[k]).wait_send()
 
     for copy in outs:
         copy.wait()
@@ -380,21 +453,20 @@
     bf16 = jnp.bfloat16
     return pl.pallas_call(
         ladder_kernel,
-        out_shape=jax.ShapeDtypeStruct((2 * SUB, q_local), bf16),
+        out_shape=jax.ShapeDtypeStruct((SUB, q_local), bf16),
         in_specs=[pl.BlockSpec(memory_space=pltpu.SMEM)] + [vmem] * 5 + [hbm] * 2,
         out_specs=hbm,
         scratch_shapes=[
-            pltpu.VMEM((8, q_local // QC, k_local, QC), bf16),
+            pltpu.VMEM((8, NQ, k_local, QC), bf16),
             pltpu.VMEM((NH, SUB, k_local), bf16),
             pltpu.VMEM((NT, T, k_local), bf16),
-            pltpu.VMEM((SUB, SUB), bf16),
             pltpu.VMEM((NP + 1, T, QC), bf16),
             pltpu.VMEM((SUB, QC), bf16),
-            pltpu.VMEM((2, SUB, q_local), bf16),
-            pltpu.VMEM((4, SUB, q_local), bf16),
-            pltpu.VMEM((2, SUB, q_local), bf16),
-            dma((8, q_local // QC)), dma((2,)), dma((NH,)), dma((4,)), dma((NH,)),
-            dma((2,)), dma((4,)), dma((2,)), dma((2,)), dma((2,)),
+            pltpu.VMEM((2, SUB, QC), bf16),
+            pltpu.VMEM((2 * NQ, SUB, QC), bf16),
+            pltpu.VMEM((NQ, SUB, QC), bf16),
+            dma((8, NQ)), dma((NT,)), dma((NH, 2)), dma((10,)),
+            dma((2,)), dma((2 * NQ,)), dma((NQ,)), dma((NQ,)), dma((NQ,)),
         ],
         compiler_params=pltpu.CompilerParams(
             collective_id=0, has_side_effects=True, vmem_limit_bytes=64 * 1024 * 1024 - 256 * 1024

time: 247 us -> 212 us (0.86); the launches traced: 242 us -> 211 us
  Pallas kernels: 226 us -> 194 us
    pallas_call x1, Pallas kernels: 226 us -> 194 us  [fused(): pl.pallas_call(ladder_kernel, out_shape=jax.ShapeDtypeStruct((SUB, q_loca...]
where the time goes in v2:
time: 212 us; the launch traced here: 211 us
  Pallas kernels  194 us (92%)
  local copies, waits for them, and re-layouts  9.03 us (4%)
  other arithmetic  7.63 us (4%)
    pallas_call x1, Pallas kernels, fused(): pl.pallas_call(ladder_kernel, out_shape=jax.ShapeDtypeStruct((SUB, q_loca...  194 us
    unnamed x3, local copies, waits for them, and re-layouts  4.79 us

profile of v2, /device:TPU:1, one launch (start us, length us, event | category | flops | bytes accessed | tf_op | source)
XLA Modules:
  0.0 211.4 jit_solution(8407873924079262948)
XLA Ops:
  0.2 0.7 xor.59
  0.9 0.7 select_reduce_fusion.4
  1.7 0.7 xor.62
  2.4 0.8 select_reduce_fusion.2
  3.3 0.8 select_reduce_fusion.3
  4.3 0.2 convert_reduce_fusion
  4.4 0.2 select_reduce_fusion.7
  4.6 0.4 fusion.12
  5.0 0.2 scatter.9.seg_ref
  5.3 0.1 copy.19
  5.4 0.1 select_reduce_fusion.6
  5.6 0.1 convert_reduce_fusion.2
  5.7 0.6 broadcast_in_dim.154.pos_ref
  6.3 2.1 %select_reduce_fusion = s32[4,1024]{1,0:T(4,128)S(1)} fusion(s32[4,1024]{1,0:T(4,128)S(1)} %fusion.12), kind=kLoop, calls=%fused_computation | loop fusion | flops 12578816 | bytes 32768 | tf_op jit(solution)/shard_map/reduce_sum | solution.py:417
  8.5 0.6 reshape.283.src_ref
  9.1 0.1 copy.20
  9.2 0.1 reshape.281
  9.3 0.7 reshape.282.tab
  10.0 0.9 select_reduce_fusion.1
  10.9 0.1 reduce_sum.131
  11.0 0.7 compare_convert_fusion.qval_ref
  11.7 0.7 pad_convert_fusion.kval_ref
  12.4 194.2 %shard_map.64 = bf16[1024,2048]{1,0:T(8,128)(2,1)} custom-call(s32[256]{0:T(256)} %reshape.282.tab, s32[4,1,1024]{2,1,0:T(1,128)} %reshape.283.src_ref, s32[4,1,1024]{2,1,0:T(1,128)} %broadcast_in_dim.154.pos_ref, s32[4,2,128]{2,1,0:T(2,128)} %copy-done, bf16[128,1024]{1,0:T(8,128)(2,1)} %pad_convert_fusion.kval_ref, ...), custom_call_target="tpu_custom_call" | custom-call | flops 47244640256 | bytes 41943040 | tf_op jit(solution)/shard_map/pallas_call | solution.py:454
  206.6 4.8 %copy.25 = bf16[1024,2048]{1,0:T(8,128)(2,1)} copy(bf16[1024,2048]{1,0:T(8,128)(2,1)} %shard_map.64) | data formatting | bytes 8388608
  (27 shorter events, 0.7 us)
Async XLA Ops:
  5.2 7.2 %copy-start = (s32[4,2,128]{2,1,0:T(2,128)}, s32[4,2,128]{2,1,0:T(2,128)S(1)}, u32[]{:S(2)}) copy-start(s32[4,2,128]{2,1,0:T(2,128)S(1)} %scatter.9.seg_ref) | copy-start | bytes 12292
